TPU v7x, 32 devices: a whole 2x2x4 slice. The times are simulated.
32 devices in a mesh: parts: 2 (over y), wide: 4 (over z), narrow: 4 (over x, core).
Axes of the slice: x: 2, y: 2, z: 4, core: 2. Of those that a mesh axis runs over, the one named last changes fastest.
Arguments:
- tokens: bfloat16 [2, 256, 7168], P(None, ('parts', 'wide', 'narrow')), parts along dimension 1, may hold values from -6 to 6
- route_copy: int32 [2, 256, 4], P(None, ('parts', 'wide', 'narrow')), parts along dimension 1, may hold values from 0 to 3, as said below
- gate_value: float32 [2, 256, 4], P(None, ('parts', 'wide', 'narrow')), parts along dimension 1, may hold values from 0.05 to 0.6
- w_gate_up: bfloat16 [16, 7168, 512], P(('wide', 'narrow')), may hold values from -0.0625 to 0.0625
- w_down: bfloat16 [16, 256, 7168], P(('wide', 'narrow')), may hold values from -0.1875 to 0.1875
Outputs:
- mixed: bfloat16 [2, 256, 7168], P(None, ('parts', 'wide', 'narrow')), parts along dimension 1
There are 2 independent parts, one for each index of `parts`. A program takes and returns all parts, laid end to end along the dimension named above; an argument that names none is the same for every part. Nothing has to cross between parts.
Inputs may be any that keep to these rules, and one draw needn't show every extreme that they name: `route_copy`: each token names 4 different copies; copy c belongs to node group c, and one token's copies lie in at most 4 node groups. Within one step the 8 tokens of one device (aligned blocks of rows) name no copy more than 8 times.
All inputs are finite; a program needn't handle non-finite values.
Results may differ from a plain program's by a relative error of at most 0.013.
Values may be sent and summed in bfloat16 or wider, within the bound.
A program may use at most 128 MiB of HBM per device.

v0:
```python
import jax
import jax.numpy as jnp
from jax import lax
from jax.sharding import PartitionSpec as P

SPLIT = 4


def from_partner(block, axis, bit):
    count = lax.axis_size(axis)
    route = []
    for low in range(count):
        high = low | 1 << bit
        if high != low and high < count:
            route += [(low, high), (high, low)]
    return lax.ppermute(block, axis, route)


def expert_block(packet, gate_up, down):
    width = down.shape[0]
    lead = packet.shape[:-1]
    row_block = packet.reshape(-1, packet.shape[-1])
    joined = jnp.dot(row_block, gate_up, preferred_element_type=jnp.float32)
    hidden = (jax.nn.silu(joined[:, :width]) * joined[:, width:]).astype(jnp.bfloat16)
    produced = jnp.dot(hidden, down, preferred_element_type=jnp.float32).astype(jnp.bfloat16)
    return produced.reshape(lead + (down.shape[1],))


def rank_pairs(route_now, copy_count):
    one_hot = (route_now[..., None] == jnp.arange(copy_count, dtype=jnp.int32)).astype(jnp.int32)
    counts = jnp.sum(one_hot, axis=-2)
    before = jnp.cumsum(counts, axis=-2) - counts
    return jnp.sum(one_hot * before[..., None, :], axis=-1)


def select_rows(target, gates, slot_total):
    matches = target[None, :, :] == jnp.arange(slot_total, dtype=jnp.int32)[:, None, None]
    picker = jnp.any(matches, axis=-1).astype(jnp.bfloat16)
    weights = jnp.sum(jnp.where(matches, gates[None, :, :], 0.0), axis=-1)
    return (picker, weights)


def body(tokens, route_copy, gate_value, w_gate_up, w_down):
    num_steps, tok_rows, model_dim = tokens.shape
    top_count = route_copy.shape[2]
    wide_count = lax.axis_size("wide")
    narrow_count = lax.axis_size("narrow")
    dev_count = wide_count * narrow_count
    copy_count = dev_count // SPLIT
    slot_cap = min(tok_rows, max(2, 3 * tok_rows * top_count // (2 * copy_count) + tok_rows // 64))
    gate_up = w_gate_up[0]
    down = w_down[0]
    results = []
    for step_index in range(num_steps):
        step_rows = tokens[step_index]
        step_route = route_copy[step_index]
        step_gate = gate_value[step_index]
        piece_rows = (slot_cap + SPLIT - 1) // SPLIT
        per_copy = SPLIT * piece_rows
        ranked = rank_pairs(step_route, copy_count)
        target = step_route * per_copy + ranked
        picker, weights = select_rows(target, step_gate, copy_count * per_copy)
        outbox = jnp.dot(picker, step_rows, preferred_element_type=jnp.float32).astype(jnp.bfloat16)
        outbox = outbox.reshape(dev_count, piece_rows, model_dim)
        received = lax.all_to_all(
            outbox, ("wide", "narrow"), split_axis=0, concat_axis=0, tiled=True
        )
        narrow_index = lax.axis_index("narrow")
        shared = received
        for bit_number in range(SPLIT.bit_length() - 1):
            other = from_partner(shared, "narrow", bit_number)
            upper = narrow_index >> bit_number & 1 == 1
            shared = jnp.where(
                upper,
                jnp.concatenate([other, shared], axis=1),
                jnp.concatenate([shared, other], axis=1),
            )
        produced = expert_block(shared[:, :slot_cap], gate_up, down)
        returned = lax.all_to_all(
            produced, ("wide", "narrow"), split_axis=0, concat_axis=0, tiled=True
        )
        summed = jnp.sum(
            returned.reshape(copy_count, SPLIT, slot_cap, model_dim).astype(jnp.float32), axis=1
        )
        used = weights.reshape(copy_count, per_copy, tok_rows)[:, :slot_cap].reshape(
            copy_count * slot_cap, tok_rows
        )
        total = jnp.dot(
            used.T,
            summed.reshape(copy_count * slot_cap, model_dim),
            precision=lax.Precision.HIGHEST,
        )
        results.append(total.astype(jnp.bfloat16))
    return jnp.stack(results)


def solution(mesh):
    return jax.shard_map(
        body,
        mesh=mesh,
        in_specs=(
            P(None, ("parts", "wide", "narrow"), None),
            P(None, ("parts", "wide", "narrow"), None),
            P(None, ("parts", "wide", "narrow"), None),
            P(("wide", "narrow"), None, None),
            P(("wide", "narrow"), None, None),
        ),
        out_specs=P(None, ("parts", "wide", "narrow"), None),
        check_vma=False,
    )
```

profile of v0, /device:TPU:11, one launch (start us, length us, event | category | flops | bytes accessed | tf_op | source)
XLA Modules:
  0.0 164.1 jit_solution(17588904577729960737)
XLA Ops:
  0.0 0.7 slice_bitcast_fusion.3
  0.9 0.7 fusion.41
  1.8 0.7 fusion.40
  2.6 1.2 convolution_convert_fusion.2
  4.0 18.5 %all_to_all.20 = bf16[16,2,7168]{2,1,0:T(2,128)(2,1)S(1)} all-to-all(bf16[16,2,7168]{2,1,0:T(2,128)(2,1)S(1)} %reshape.75), channel_id=1, replica_groups=mesh['parts'=2,'wide'=4,'narrow'=4] {'wide','narrow'}, dimensions={0} | all-to-all | bytes 917504 | tf_op jit(solution)/shard_map/all_to_all | solution.py:65
  22.8 1.6 collective-permute-done.2
  24.4 1.7 %maximum_select_fusion.3 = bf16[16,4,7168]{2,1,0:T(4,128)(2,1)S(1)} fusion(bf16[16,2,7168]{2,1,0:T(2,128)(2,1)S(1)} %all_to_all.20, bf16[16,2,7168]{2,1,0:T(2,128)(2,1)S(1)} %collective-permute-done.2, pred[]{:T(512)S(6)} %eq.77), kind=kLoop, calls=%fused_computation.35 | loop fusion | flops 4128768 | bytes 1835009 | tf_op jit(solution)/shard_map/jit(_where)/select_n | solution.py:73
  26.0 0.9 collective-permute-start.3
  27.4 1.0 reshape.72
  28.3 5.1 %all-to-all-start = ((bf16[16,2,7168]{2,1,0:T(2,128)(2,1)}), bf16[16,2,7168]{2,1,0:T(2,128)(2,1)S(1)}, u32[]{:S(2)}, u32[]{:S(2)}) async-start(bf16[16,2,7168]{2,1,0:T(2,128)(2,1)} %reshape.72), calls=%async_computation | async-start | bytes 917504 | tf_op jit(solution)/shard_map/all_to_all | solution.py:65
  33.5 18.1 %collective-permute-done.3 = bf16[16,4,7168]{2,1,0:T(4,128)(2,1)S(1)} collective-permute-done((bf16[16,4,7168]{2,1,0:T(4,128)(2,1)S(1)}, bf16[16,4,7168]{2,1,0:T(4,128)(2,1)S(1)}, u32[]{:S(2)}, u32[]{:S(2)}) %collective-permute-start.3) | collective-permute-done | bytes 917536 | tf_op jit(solution)/shard_map/ppermute | solution.py:16
  51.5 5.0 %fusion.4 = f32[128,512]{1,0:T(8,128)S(1)} fusion(bf16[1,7168,512]{2,1,0:T(8,128)(2,1)} %param.8, bf16[16,4,7168]{2,1,0:T(4,128)(2,1)S(1)} %maximum_select_fusion.3, bf16[16,4,7168]{2,1,0:T(4,128)(2,1)S(1)} %collective-permute-done.3, pred[]{:T(512)S(6)} %eq.76), kind=kOutput, calls=%fused_computation.10 | convolution fusion | flops 947781632 | bytes 9437185 | tf_op jit(solution)/shard_map/dot_general | solution.py:23
  56.5 1.9 %fusion.1 = bf16[16,8,7168]{2,1,0:T(8,128)(2,1)} fusion(bf16[1,256,7168]{2,1,0:T(8,128)(2,1)S(1)} %copy-done, f32[128,512]{1,0:T(8,128)S(1)} %fusion.4), kind=kOutput, calls=%fused_computation.3 | convolution fusion | flops 470876160 | bytes 5767168 | tf_op jit(solution)/shard_map/dot_general | solution.py:25
  58.4 6.4 %all-to-all-start.3 = ((bf16[16,8,7168]{2,1,0:T(8,128)(2,1)}), bf16[16,8,7168]{2,1,0:T(8,128)(2,1)S(1)}, u32[]{:S(2)}, u32[]{:S(2)}) async-start(bf16[16,8,7168]{2,1,0:T(8,128)(2,1)} %fusion.1), calls=%async_computation.3 | async-start | bytes 3670016 | tf_op jit(solution)/shard_map/all_to_all | solution.py:79
  65.2 1.5 collective-permute-done
  66.7 1.7 %maximum_select_fusion.2 = bf16[16,4,7168]{2,1,0:T(4,128)(2,1)S(1)} fusion(bf16[16,2,7168]{2,1,0:T(2,128)(2,1)S(1)} %all-to-all-done, bf16[16,2,7168]{2,1,0:T(2,128)(2,1)S(1)} %collective-permute-done, pred[]{:T(512)S(6)} %eq.77), kind=kLoop, calls=%fused_computation.34 | loop fusion | flops 4128768 | bytes 1835009 | tf_op jit(solution)/shard_map/jit(_where)/select_n | solution.py:73
  68.7 35.6 %collective-permute-done.1 = bf16[16,4,7168]{2,1,0:T(4,128)(2,1)S(1)} collective-permute-done((bf16[16,4,7168]{2,1,0:T(4,128)(2,1)S(1)}, bf16[16,4,7168]{2,1,0:T(4,128)(2,1)S(1)}, u32[]{:S(2)}, u32[]{:S(2)}) %collective-permute-start.1) | collective-permute-done | bytes 917536 | tf_op jit(solution)/shard_map/ppermute | solution.py:16
  104.2 5.1 %fusion.6 = f32[128,512]{1,0:T(8,128)S(1)} fusion(bf16[1,7168,512]{2,1,0:T(8,128)(2,1)} %param.8, bf16[16,4,7168]{2,1,0:T(4,128)(2,1)S(1)} %maximum_select_fusion.2, bf16[16,4,7168]{2,1,0:T(4,128)(2,1)S(1)} %collective-permute-done.1, pred[]{:T(512)S(6)} %eq.76), kind=kOutput, calls=%fused_computation.12 | convolution fusion | flops 947781632 | bytes 9437185 | tf_op jit(solution)/shard_map/dot_general | solution.py:23
  109.3 1.9 %fusion = bf16[16,8,7168]{2,1,0:T(8,128)(2,1)} fusion(bf16[1,256,7168]{2,1,0:T(8,128)(2,1)S(1)} %copy-done.1, f32[128,512]{1,0:T(8,128)S(1)} %fusion.6), kind=kOutput, calls=%fused_computation.2 | convolution fusion | flops 470876160 | bytes 5767168 | tf_op jit(solution)/shard_map/dot_general | solution.py:25
  111.2 7.8 %all-to-all-start.1 = ((bf16[16,8,7168]{2,1,0:T(8,128)(2,1)}), bf16[16,8,7168]{2,1,0:T(8,128)(2,1)}, u32[]{:S(2)}, u32[]{:S(2)}) async-start(bf16[16,8,7168]{2,1,0:T(8,128)(2,1)} %fusion), calls=%async_computation.1 | async-start | bytes 3670016 | tf_op jit(solution)/shard_map/all_to_all | solution.py:79
  119.4 0.5 fusion.3
  120.0 41.0 %all-to-all-done.1 = bf16[16,8,7168]{2,1,0:T(8,128)(2,1)} async-done(((bf16[16,8,7168]{2,1,0:T(8,128)(2,1)}), bf16[16,8,7168]{2,1,0:T(8,128)(2,1)}, u32[]{:S(2)}, u32[]{:S(2)}) %all-to-all-start.1) | async-done | bytes 1835040 | tf_op jit(solution)/shard_map/all_to_all | solution.py:79
  161.0 1.9 %convert_reduce_fusion.1 = f32[4,8,7168]{2,1,0:T(8,128)S(1)} fusion(bf16[16,8,7168]{2,1,0:T(8,128)(2,1)} %all-to-all-done.1), kind=kLoop, calls=%fused_computation.15 | loop fusion | flops 1605632 | bytes 2752512 | tf_op jit(solution)/shard_map/reduce_sum | solution.py:82
  163.4 0.7 pad_maximum_fusion
  (29 shorter events, 3.0 us)
Async XLA Ops:
  3.8 23.2 %copy-start.2 = (bf16[2,8,7168]{2,1,0:T(8,128)(2,1)S(1)}, bf16[2,8,7168]{2,1,0:T(8,128)(2,1)}, u32[]{:S(2)}) copy-start(bf16[2,8,7168]{2,1,0:T(8,128)(2,1)} %param.5) | copy-start | bytes 688132
  22.5 1.8 %collective-permute-start.2 = (bf16[16,2,7168]{2,1,0:T(2,128)(2,1)S(1)}, bf16[16,2,7168]{2,1,0:T(2,128)(2,1)S(1)}, u32[]{:S(2)}, u32[]{:S(2)}) collective-permute-start(bf16[16,2,7168]{2,1,0:T(2,128)(2,1)S(1)} %all_to_all.20), channel_id=1, source_target_pairs={{0,1},{1,0},{2,3},{3,2},{4,5},{5,4},{6,7},{7,6},{8,9},{9,8},{10,11... | collective-permute-start | bytes 1376264 | tf_op jit(solution)/shard_map/ppermute | solution.py:16
  26.0 25.5 %collective-permute-start.3 = (bf16[16,4,7168]{2,1,0:T(4,128)(2,1)S(1)}, bf16[16,4,7168]{2,1,0:T(4,128)(2,1)S(1)}, u32[]{:S(2)}, u32[]{:S(2)}) collective-permute-start(bf16[16,4,7168]{2,1,0:T(4,128)(2,1)S(1)} %maximum_select_fusion.3), channel_id=1, source_target_pairs={{0,2},{2,0},{1,3},{3,1},{4,6},{6,4},{5,7},{7,5},{8,10},{10,8},{9,1... | collective-permute-start | bytes 2752520 | tf_op jit(solution)/shard_map/ppermute | solution.py:16
  28.3 30.1 %all-to-all-start = ((bf16[16,2,7168]{2,1,0:T(2,128)(2,1)}), bf16[16,2,7168]{2,1,0:T(2,128)(2,1)S(1)}, u32[]{:S(2)}, u32[]{:S(2)}) async-start(bf16[16,2,7168]{2,1,0:T(2,128)(2,1)} %reshape.72), calls=%async_computation | async-start | bytes 917504 | tf_op jit(solution)/shard_map/all_to_all | solution.py:65
  51.5 5.0 %copy-start = (bf16[1,256,7168]{2,1,0:T(8,128)(2,1)S(1)}, bf16[1,256,7168]{2,1,0:T(8,128)(2,1)}, u32[]{:S(2)}) copy-start(bf16[1,256,7168]{2,1,0:T(8,128)(2,1)} %param.9) | copy-start | bytes 11010052
  58.4 52.8 %all-to-all-start.3 = ((bf16[16,8,7168]{2,1,0:T(8,128)(2,1)}), bf16[16,8,7168]{2,1,0:T(8,128)(2,1)S(1)}, u32[]{:S(2)}, u32[]{:S(2)}) async-start(bf16[16,8,7168]{2,1,0:T(8,128)(2,1)} %fusion.1), calls=%async_computation.3 | async-start | bytes 3670016 | tf_op jit(solution)/shard_map/all_to_all | solution.py:79
  64.8 1.8 %collective-permute-start = (bf16[16,2,7168]{2,1,0:T(2,128)(2,1)S(1)}, bf16[16,2,7168]{2,1,0:T(2,128)(2,1)S(1)}, u32[]{:S(2)}, u32[]{:S(2)}) collective-permute-start(bf16[16,2,7168]{2,1,0:T(2,128)(2,1)S(1)} %all-to-all-done), channel_id=1, source_target_pairs={{0,1},{1,0},{2,3},{3,2},{4,5},{5,4},{6,7},{7,6},{8,9},{9,8},{10,11... | collective-permute-start | bytes 1376264 | tf_op jit(solution)/shard_map/ppermute | solution.py:16
  68.3 35.9 %collective-permute-start.1 = (bf16[16,4,7168]{2,1,0:T(4,128)(2,1)S(1)}, bf16[16,4,7168]{2,1,0:T(4,128)(2,1)S(1)}, u32[]{:S(2)}, u32[]{:S(2)}) collective-permute-start(bf16[16,4,7168]{2,1,0:T(4,128)(2,1)S(1)} %maximum_select_fusion.2), channel_id=1, source_target_pairs={{0,2},{2,0},{1,3},{3,1},{4,6},{6,4},{5,7},{7,5},{8,10},{10,8},{9,1... | collective-permute-start | bytes 2752520 | tf_op jit(solution)/shard_map/ppermute | solution.py:16
  104.2 5.1 %copy-start.1 = (bf16[1,256,7168]{2,1,0:T(8,128)(2,1)S(1)}, bf16[1,256,7168]{2,1,0:T(8,128)(2,1)}, u32[]{:S(2)}) copy-start(bf16[1,256,7168]{2,1,0:T(8,128)(2,1)} %param.9) | copy-start | bytes 11010052
  111.2 7.9 %copy-start.3 = (f32[2,8,4]{1,2,0:T(4,128)S(1)}, f32[2,8,4]{1,2,0:T(4,128)}, u32[]{:S(2)}) copy-start(f32[2,8,4]{1,2,0:T(4,128)} %param.7) | copy-start | bytes 772
  111.2 49.8 %all-to-all-start.1 = ((bf16[16,8,7168]{2,1,0:T(8,128)(2,1)}), bf16[16,8,7168]{2,1,0:T(8,128)(2,1)}, u32[]{:S(2)}, u32[]{:S(2)}) async-start(bf16[16,8,7168]{2,1,0:T(8,128)(2,1)} %fusion), calls=%async_computation.1 | async-start | bytes 3670016 | tf_op jit(solution)/shard_map/all_to_all | solution.py:79
where the time goes:
time: 165 us; the launch traced here: 164 us
  waiting for transfers between devices  97.7 us (59%)
  starting transfers between devices  21.2 us (13%)
  blocking collectives  18.5 us (11%)
  matrix products  16.5 us (10%)
  other arithmetic  8.27 us (5%)
  local copies, waits for them, and re-layouts  1.83 us (1%)
    ppermute x4, waiting for transfers between devices, from_partner(): return lax.ppermute(block, axis, route)  56.7 us
    all_to_all x2, waiting for transfers between devices, body(): lax.all_to_all(produced, ('wide', 'narrow'), split_axis=0, concat_axis=0,...  41 us
    all_to_all x1, blocking collectives, body(): lax.all_to_all(outbox, ('wide', 'narrow'), split_axis=0, concat_axis=0, t...  18.5 us
    all_to_all x2, starting transfers between devices, body(): lax.all_to_all(produced, ('wide', 'narrow'), split_axis=0, concat_axis=0,...  14.3 us
    dot_general x2, matrix products, expert_block(): joined = jnp.dot(row_block, gate_up, preferred_element_type=jnp.float32)  10 us
    all_to_all x1, starting transfers between devices, body(): lax.all_to_all(outbox, ('wide', 'narrow'), split_axis=0, concat_axis=0, t...  5.13 us
    dot_general x2, matrix products, expert_block(): jnp.dot(hidden, down, preferred_element_type=jnp.float32)  3.83 us
    select_n x2, other arithmetic, body(): jnp.where(upper, jnp.concatenate([other, shared], axis=1), jnp.concatenat...  3.31 us
  transfers between devices with their start and end apart: 7, of which 5 were waited for; matrix products, arithmetic and copies ran while one was open for 11% of the time, Pallas kernels for 0%

commit v1 on v0

--- a/solution.py
+++ b/solution.py
@@ -1,6 +1,10 @@
+import functools
+
 import jax
 import jax.numpy as jnp
 from jax import lax
+from jax.experimental import pallas as pl
+from jax.experimental.pallas import tpu as pltpu
 from jax.sharding import PartitionSpec as P
 
 SPLIT = 4
@@ -94,9 +98,268 @@
     return jnp.stack(results)
 
 
+NUM_CHUNKS = 4
+LANES = 128
+THIRD = 32
+MESH = pl.DeviceIdType.MESH
+
+
+def dense_kernel(
+    wide_count, tok_ref, route_ref, gate_ref, up_hbm, down_hbm, out_ref,
+    held, up, down, acc, hid, core_out, core_in, core_own, x_out, x_in, x_own, z_out, z_in,
+    up_sem, down_sem, gz_s, gz_r, gx_s, gx_r, ga_s, ga_r, gb_s, gb_r,
+    rc_s, rc_r, rx_s, rx_r, rz_s, rz_r,
+):
+    rows, dim = tok_ref.shape
+    width = down.shape[0]
+    size = dim // NUM_CHUNKS
+    part = lax.axis_index("parts")
+    z = lax.axis_index("wide")
+    narrow = lax.axis_index("narrow")
+    x = narrow // 2
+    c = narrow % 2
+    x_peer = (part, z, (1 - x) * 2 + c)
+    c_peer = (part, z, x * 2 + 1 - c)
+    offsets = list(range(1, wide_count))
+    z_peers = {k: lax.rem(z + k, wide_count) for k in offsets}
+    z_from = {k: lax.rem(z + wide_count - k, wide_count) for k in offsets}
+    z_from[0] = z
+
+    def block(index):
+        return pl.ds(pl.multiple_of(index * rows, rows), rows)
+
+    def held_cols(ch):
+        if ch == 0:
+            return pl.ds(0, LANES + size)
+        return pl.ds(LANES + ch * size, size)
+
+    up_copies = []
+    for ch in range(NUM_CHUNKS):
+        span = pl.ds(ch * size, size)
+        copy = pltpu.make_async_copy(up_hbm.at[span], up.at[span], up_sem.at[ch])
+        copy.start()
+        up_copies.append(copy)
+    down_copy = pltpu.make_async_copy(down_hbm, down, down_sem)
+    down_copy.start()
+
+    barrier = pltpu.get_barrier_semaphore()
+    peers = [(part, z_peers[k], narrow) for k in offsets] + [x_peer, c_peer]
+    for peer in peers:
+        pl.semaphore_signal(barrier, inc=1, device_id=peer, device_id_type=MESH)
+
+    lane = lax.broadcasted_iota(jnp.int32, (rows, LANES), 1)
+    weight = jnp.zeros((rows, LANES), jnp.float32)
+    for k in range(route_ref.shape[1]):
+        weight += jnp.where(lane % THIRD == route_ref[:, k : k + 1], gate_ref[:, k : k + 1], 0.0)
+    high = weight.astype(jnp.bfloat16).astype(jnp.float32)
+    mid = (weight - high).astype(jnp.bfloat16).astype(jnp.float32)
+    low = weight - high - mid
+    coded = jnp.where(
+        lane < THIRD, high, jnp.where(lane < 2 * THIRD, mid, jnp.where(lane < 3 * THIRD, low, 0.0))
+    )
+    held[x, c, block(z), 0:LANES] = coded.astype(jnp.bfloat16)
+    held[x, c, block(z), LANES:] = tok_ref[...]
+
+    pl.semaphore_wait(barrier, len(peers))
+
+    sends = []
+
+    def remote(src, dst, send_sem, recv_sem, peer):
+        copy = pltpu.make_async_remote_copy(
+            src_ref=src, dst_ref=dst, send_sem=send_sem, recv_sem=recv_sem,
+            device_id=peer, device_id_type=MESH,
+        )
+        sends.append(copy)
+        return copy
+
+    z_copy, x_copy, a_copy, b_copy = {}, {}, {}, {}
+    for ch in range(NUM_CHUNKS):
+        own = held.at[x, c, block(z), held_cols(ch)]
+        for k in offsets:
+            z_copy[ch, k] = remote(
+                own, own, gz_s.at[ch, k], gz_r.at[ch, k], (part, z_peers[k], narrow)
+            )
+            z_copy[ch, k].start()
+        x_copy[ch, 0] = remote(own, own, gx_s.at[ch, 0], gx_r.at[ch, 0], x_peer)
+        x_copy[ch, 0].start()
+
+    def gather_a(ch):
+        for k in offsets:
+            z_copy[ch, k].wait_recv()
+            ref = held.at[x, c, block(z_from[k]), held_cols(ch)]
+            x_copy[ch, k] = remote(ref, ref, gx_s.at[ch, k], gx_r.at[ch, k], x_peer)
+            x_copy[ch, k].start()
+        ref = held.at[x, c, :, held_cols(ch)]
+        a_copy[ch] = remote(ref, ref, ga_s.at[ch], ga_r.at[ch], c_peer)
+        a_copy[ch].start()
+
+    def gather_b(ch):
+        for k in [0] + offsets:
+            x_copy[ch, k].wait_recv()
+        ref = held.at[1 - x, c, :, held_cols(ch)]
+        b_copy[ch] = remote(ref, ref, gb_s.at[ch], gb_r.at[ch], c_peer)
+        b_copy[ch].start()
+
+    def gather_c(ch):
+        a_copy[ch].wait_recv()
+        b_copy[ch].wait_recv()
+        up_copies[ch].wait()
+        cols = held[:, :, :, LANES + ch * size : LANES + (ch + 1) * size]
+        term = jnp.dot(
+            cols.reshape(-1, size), up[ch * size : (ch + 1) * size, :],
+            preferred_element_type=jnp.float32,
+        )
+        if ch == 0:
+            acc[...] = term
+        else:
+            acc[...] += term
+
+    for i in range(NUM_CHUNKS + 2):
+        if i < NUM_CHUNKS:
+            gather_a(i)
+        if 0 <= i - 1 < NUM_CHUNKS:
+            gather_b(i - 1)
+        if 0 <= i - 2:
+            gather_c(i - 2)
+
+    joined = acc[...]
+    gate = joined[:, :width]
+    value = gate / (1.0 + jnp.exp(-gate)) * joined[:, width:]
+    hid[...] = value.astype(jnp.bfloat16).reshape(hid.shape)
+    down_copy.wait()
+
+    def row_weights(core):
+        coded = held[:, core, :, 0:LANES].reshape(-1, LANES).astype(jnp.float32)
+        lane = lax.broadcasted_iota(jnp.int32, coded.shape, 1)
+        return jnp.sum(jnp.where(lane % THIRD == z, coded, 0.0), axis=1, keepdims=True)
+
+    other_weight = row_weights(1 - c)
+    own_weight = row_weights(c)
+    half = (2, wide_count * rows, size)
+    rc, rx, rz = {}, {}, {}
+
+    def scatter_a(ch):
+        cols = slice(ch * size, (ch + 1) * size)
+        out = jnp.dot(
+            hid[:, 1 - c].reshape(-1, width), down[:, cols], preferred_element_type=jnp.float32
+        )
+        core_out[ch] = (out * other_weight).astype(jnp.bfloat16).reshape(half)
+        rc[ch] = remote(core_out.at[ch], core_in.at[ch], rc_s.at[ch], rc_r.at[ch], c_peer)
+        rc[ch].start()
+        out = jnp.dot(
+            hid[:, c].reshape(-1, width), down[:, cols], preferred_element_type=jnp.float32
+        )
+        core_own[ch] = (out * own_weight).reshape(half)
+
+    def scatter_b(ch):
+        rc[ch].wait_recv()
+        out = core_own[ch, 1 - x] + core_in[ch, 1 - x].astype(jnp.float32)
+        x_out[ch] = out.astype(jnp.bfloat16)
+        rx[ch] = remote(x_out.at[ch], x_in.at[ch], rx_s.at[ch], rx_r.at[ch], x_peer)
+        rx[ch].start()
+        x_own[ch] = core_own[ch, x] + core_in[ch, x].astype(jnp.float32)
+
+    def scatter_c(ch):
+        rx[ch].wait_recv()
+        out = x_own[ch] + x_in[ch].astype(jnp.float32)
+        x_own[ch] = out
+        z_out[ch] = out.astype(jnp.bfloat16)
+        for k in offsets:
+            rz[ch, k] = remote(
+                z_out.at[ch, block(z_peers[k])], z_in.at[ch, k - 1],
+                rz_s.at[ch, k], rz_r.at[ch, k], (part, z_peers[k], narrow),
+            )
+            rz[ch, k].start()
+
+    def scatter_d(ch):
+        out = x_own[ch, block(z), :]
+        for k in offsets:
+            rz[ch, k].wait_recv()
+            out += z_in[ch, k - 1].astype(jnp.float32)
+        out_ref[:, ch * size : (ch + 1) * size] = out.astype(jnp.bfloat16)
+
+    for i in range(NUM_CHUNKS + 1):
+        if i < NUM_CHUNKS:
+            scatter_a(i)
+        if 0 <= i - 1:
+            scatter_b(i - 1)
+    for i in range(NUM_CHUNKS + 1):
+        if i < NUM_CHUNKS:
+            scatter_c(i)
+        if 0 <= i - 1:
+            scatter_d(i - 1)
+    for copy in sends:
+        copy.wait_send()
+
+
+def dense_body(tokens, route_copy, gate_value, w_gate_up, w_down):
+    num_steps, tok_rows, dim = tokens.shape
+    rows = num_steps * tok_rows
+    wide_count = lax.axis_size("wide")
+    width = w_down.shape[1]
+    size = dim // NUM_CHUNKS
+    col = wide_count * rows
+    bf16, f32 = jnp.bfloat16, jnp.float32
+    vmem = pl.BlockSpec(memory_space=pltpu.VMEM)
+    hbm = pl.BlockSpec(memory_space=pl.ANY)
+    dma = pltpu.SemaphoreType.DMA
+    n = NUM_CHUNKS
+    out = pl.pallas_call(
+        functools.partial(dense_kernel, wide_count),
+        out_shape=jax.ShapeDtypeStruct((rows, dim), bf16),
+        in_specs=[vmem, vmem, vmem, hbm, hbm],
+        out_specs=vmem,
+        scratch_shapes=[
+            pltpu.VMEM((2, 2, col, LANES + dim), bf16),
+            pltpu.VMEM((dim, 2 * width), bf16),
+            pltpu.VMEM((width, dim), bf16),
+            pltpu.VMEM((4 * col, 2 * width), f32),
+            pltpu.VMEM((2, 2, col, width), bf16),
+            pltpu.VMEM((n, 2, col, size), bf16),
+            pltpu.VMEM((n, 2, col, size), bf16),
+            pltpu.VMEM((n, 2, col, size), f32),
+            pltpu.VMEM((n, col, size), bf16),
+            pltpu.VMEM((n, col, size), bf16),
+            pltpu.VMEM((n, col, size), f32),
+            pltpu.VMEM((n, col, size), bf16),
+            pltpu.VMEM((n, wide_count - 1, rows, size), bf16),
+            dma((n,)), dma,
+            dma((n, wide_count)), dma((n, wide_count)),
+            dma((n, wide_count)), dma((n, wide_count)),
+            dma((n,)), dma((n,)), dma((n,)), dma((n,)),
+            dma((n,)), dma((n,)), dma((n,)), dma((n,)),
+            dma((n, wide_count)), dma((n, wide_count)),
+        ],
+        compiler_params=pltpu.CompilerParams(
+            collective_id=0, has_side_effects=True, vmem_limit_bytes=56 * 1024 * 1024
+        ),
+        cost_estimate=pl.CostEstimate(
+            flops=12 * col * dim * width * 2, bytes_accessed=3 * dim * width * 2, transcendentals=0
+        ),
+    )(
+        tokens.reshape(rows, dim),
+        route_copy.reshape(rows, -1),
+        gate_value.reshape(rows, -1),
+        w_gate_up[0],
+        w_down[0],
+    )
+    return out.reshape(num_steps, tok_rows, dim)
+
+
+def choose_body(tokens, route_copy, gate_value, w_gate_up, w_down):
+    wide_count = lax.axis_size("wide")
+    narrow_count = lax.axis_size("narrow")
+    copy_count = wide_count * narrow_count // SPLIT
+    every_copy = route_copy.shape[2] == copy_count and copy_count <= THIRD
+    whole_rows = tokens.shape[0] * tokens.shape[1] % 16 == 0
+    if every_copy and whole_rows and narrow_count == SPLIT:
+        return dense_body(tokens, route_copy, gate_value, w_gate_up, w_down)
+    return body(tokens, route_copy, gate_value, w_gate_up, w_down)
+
+
 def solution(mesh):
     return jax.shard_map(
-        body,
+        choose_body,
         mesh=mesh,
         in_specs=(
             P(None, ("parts", "wide", "narrow"), None),

time: 165 us -> 70.4 us (0.43)
  the two profiles are of different devices: /device:TPU:11 before, /device:TPU:0 now
where the time goes in v1:
time: 70.4 us; the launch traced here: 70.2 us
  Pallas kernels  65.8 us (93%)
  local copies, waits for them, and re-layouts  4.37 us (6%)
    pallas_call x1, Pallas kernels, dense_body(): pl.pallas_call(functools.partial(dense_kernel, wide_count), out_shape=jax...  65.8 us
    unnamed x1, local copies, waits for them, and re-layouts  1.64 us

profile of v1, /device:TPU:0, one launch (start us, length us, event | category | flops | bytes accessed | tf_op | source)
XLA Modules:
  0.0 70.2 jit_solution(472113675878011465)
XLA Ops:
  0.0 1.4 %copy.10 = s32[2,8,4]{2,1,0:T(8,128)} copy(s32[2,8,4]{1,2,0:T(4,128)} %param.6) | data formatting | bytes 512 | tf_op jit(solution)/shard_map/reshape | solution.py:341
  1.4 1.4 %copy.11 = f32[2,8,4]{2,1,0:T(8,128)} copy(f32[2,8,4]{1,2,0:T(4,128)} %param.7) | data formatting | bytes 512 | tf_op jit(solution)/shard_map/reshape | solution.py:342
  2.7 65.8 %shard_map.55 = bf16[16,7168]{1,0:T(8,128)(2,1)} custom-call(bf16[16,7168]{1,0:T(8,128)(2,1)} %bitcast.9, s32[16,4]{1,0:T(8,128)} %bitcast.10, f32[16,4]{1,0:T(8,128)} %bitcast.11, bf16[7168,512]{1,0:T(8,128)(2,1)} %bitcast.6, bf16[256,7168]{1,0:T(8,128)(2,1)} %bitcast.7), custom_call_target="tpu_custom_call" | custom-call | flops 2818572288 | bytes 11010048 | tf_op jit(solution)/shard_map/pallas_call | solution.py:307
  68.5 1.6 %copy.15 = bf16[2,8,7168]{2,1,0:T(8,128)(2,1)} copy(bf16[2,8,7168]{2,1,0:T(8,128)(2,1)} %bitcast.8) | data formatting | bytes 458752

commit v2 on v1

--- a/solution.py
+++ b/solution.py
@@ -99,6 +99,7 @@
 
 
 NUM_CHUNKS = 4
+CROSS_FIRST = (3,)
 LANES = 128
 THIRD = 32
 MESH = pl.DeviceIdType.MESH
@@ -107,10 +108,12 @@
 def dense_kernel(
     wide_count, tok_ref, route_ref, gate_ref, up_hbm, down_hbm, out_ref,
     held, up, down, acc, hid, core_out, core_in, core_own, x_out, x_in, x_own, z_out, z_in,
+    last_out, last_in,
     up_sem, down_sem, gz_s, gz_r, gx_s, gx_r, ga_s, ga_r, gb_s, gb_r,
     rc_s, rc_r, rx_s, rx_r, rz_s, rz_r,
 ):
     rows, dim = tok_ref.shape
+    num_steps, top_count, tok_rows = route_ref.shape
     width = down.shape[0]
     size = dim // NUM_CHUNKS
     part = lax.axis_index("parts")
@@ -120,18 +123,21 @@
     c = narrow % 2
     x_peer = (part, z, (1 - x) * 2 + c)
     c_peer = (part, z, x * 2 + 1 - c)
-    offsets = list(range(1, wide_count))
-    z_peers = {k: lax.rem(z + k, wide_count) for k in offsets}
-    z_from = {k: lax.rem(z + wide_count - k, wide_count) for k in offsets}
-    z_from[0] = z
+    end = wide_count - 1
+    has_low, has_high = z > 0, z < end
+    signs = (1, -1)
+    steps = [(h, s) for h in range(end) for s in range(2)]
 
     def block(index):
         return pl.ds(pl.multiple_of(index * rows, rows), rows)
 
-    def held_cols(ch):
+    def cols_of(ch):
         if ch == 0:
             return pl.ds(0, LANES + size)
         return pl.ds(LANES + ch * size, size)
+
+    def z_peer(s):
+        return (part, z + signs[s], narrow)
 
     up_copies = []
     for ch in range(NUM_CHUNKS):
@@ -143,66 +149,132 @@
     down_copy.start()
 
     barrier = pltpu.get_barrier_semaphore()
-    peers = [(part, z_peers[k], narrow) for k in offsets] + [x_peer, c_peer]
-    for peer in peers:
+
+    def greet(peer):
         pl.semaphore_signal(barrier, inc=1, device_id=peer, device_id_type=MESH)
 
-    lane = lax.broadcasted_iota(jnp.int32, (rows, LANES), 1)
-    weight = jnp.zeros((rows, LANES), jnp.float32)
-    for k in range(route_ref.shape[1]):
-        weight += jnp.where(lane % THIRD == route_ref[:, k : k + 1], gate_ref[:, k : k + 1], 0.0)
-    high = weight.astype(jnp.bfloat16).astype(jnp.float32)
-    mid = (weight - high).astype(jnp.bfloat16).astype(jnp.float32)
-    low = weight - high - mid
-    coded = jnp.where(
-        lane < THIRD, high, jnp.where(lane < 2 * THIRD, mid, jnp.where(lane < 3 * THIRD, low, 0.0))
+    pl.when(has_high)(lambda: greet(z_peer(0)))
+    pl.when(has_low)(lambda: greet(z_peer(1)))
+    greet(x_peer)
+    greet(c_peer)
+
+    eye = lax.broadcasted_iota(jnp.int32, (tok_rows, tok_rows), 0) == lax.broadcasted_iota(
+        jnp.int32, (tok_rows, tok_rows), 1
     )
-    held[x, c, block(z), 0:LANES] = coded.astype(jnp.bfloat16)
+    lane = lax.broadcasted_iota(jnp.int32, (tok_rows, LANES), 1)
+    coded_steps = []
+    for step in range(num_steps):
+        weight = jnp.zeros((tok_rows, LANES), jnp.float32)
+        for k in range(top_count):
+            route = jnp.where(eye, route_ref[step, k : k + 1, :], 0)
+            route = jnp.sum(route, axis=1, keepdims=True)
+            gate = jnp.where(eye, gate_ref[step, k : k + 1, :], 0.0)
+            gate = jnp.sum(gate, axis=1, keepdims=True)
+            weight += jnp.where(lane % THIRD == route, gate, 0.0)
+        high = weight.astype(jnp.bfloat16).astype(jnp.float32)
+        mid = (weight - high).astype(jnp.bfloat16).astype(jnp.float32)
+        low = weight - high - mid
+        low = jnp.where(lane < 3 * THIRD, low, 0.0)
+        coded_steps.append(jnp.where(lane < THIRD, high, jnp.where(lane < 2 * THIRD, mid, low)))
+    coded = jnp.concatenate(coded_steps, axis=0).astype(jnp.bfloat16)
+    held[x, c, block(z), 0:LANES] = coded
     held[x, c, block(z), LANES:] = tok_ref[...]
 
-    pl.semaphore_wait(barrier, len(peers))
+    pl.semaphore_wait(barrier, 2 + has_low.astype(jnp.int32) + has_high.astype(jnp.int32))
 
     sends = []
 
     def remote(src, dst, send_sem, recv_sem, peer):
-        copy = pltpu.make_async_remote_copy(
+        return pltpu.make_async_remote_copy(
             src_ref=src, dst_ref=dst, send_sem=send_sem, recv_sem=recv_sem,
             device_id=peer, device_id_type=MESH,
         )
-        sends.append(copy)
-        return copy
-
-    z_copy, x_copy, a_copy, b_copy = {}, {}, {}, {}
+
+    def launch(make, *cond):
+        def go():
+            make().start()
+
+        def finish():
+            make().wait_send()
+
+        if cond:
+            pl.when(cond[0])(go)
+            sends.append(lambda: pl.when(cond[0])(finish))
+        else:
+            go()
+            sends.append(finish)
+
+    def can_recv(h, s):
+        return z >= h + 1 if s == 0 else z + h + 1 <= end
+
+    def can_send(h, s):
+        return (z >= h) & has_high if s == 0 else (z + h <= end) & has_low
+
+    def z_ref(ch, index):
+        if ch in CROSS_FIRST:
+            return held.at[:, c, block(index), cols_of(ch)]
+        return held.at[x, c, block(index), cols_of(ch)]
+
+    def stream(ch, h, s):
+        ref = z_ref(ch, z - signs[s] * h)
+        return remote(ref, ref, gz_s.at[ch, s, h], gz_r.at[ch, s, h], z_peer(s))
+
+    def arrival(ch, h, s):
+        ref = z_ref(ch, z - signs[s] * (h + 1))
+        return remote(ref, ref, gz_s.at[ch, s, h], gz_r.at[ch, s, h], x_peer)
+
+    def own_x(ch):
+        ref = held.at[x, c, block(z), cols_of(ch)]
+        return remote(ref, ref, gx_s.at[ch, 2, 0], gx_r.at[ch, 2, 0], x_peer)
+
+    def forward_x(ch, h, s):
+        ref = held.at[x, c, block(z - signs[s] * (h + 1)), cols_of(ch)]
+        return remote(ref, ref, gx_s.at[ch, s, h], gx_r.at[ch, s, h], x_peer)
+
+    def core_a(ch):
+        if ch in CROSS_FIRST:
+            ref = held.at[:, c, :, cols_of(ch)]
+        else:
+            ref = held.at[x, c, :, cols_of(ch)]
+        return remote(ref, ref, ga_s.at[ch], ga_r.at[ch], c_peer)
+
+    def core_b(ch):
+        ref = held.at[1 - x, c, :, cols_of(ch)]
+        return remote(ref, ref, gb_s.at[ch], gb_r.at[ch], c_peer)
+
     for ch in range(NUM_CHUNKS):
-        own = held.at[x, c, block(z), held_cols(ch)]
-        for k in offsets:
-            z_copy[ch, k] = remote(
-                own, own, gz_s.at[ch, k], gz_r.at[ch, k], (part, z_peers[k], narrow)
-            )
-            z_copy[ch, k].start()
-        x_copy[ch, 0] = remote(own, own, gx_s.at[ch, 0], gx_r.at[ch, 0], x_peer)
-        x_copy[ch, 0].start()
-
-    def gather_a(ch):
-        for k in offsets:
-            z_copy[ch, k].wait_recv()
-            ref = held.at[x, c, block(z_from[k]), held_cols(ch)]
-            x_copy[ch, k] = remote(ref, ref, gx_s.at[ch, k], gx_r.at[ch, k], x_peer)
-            x_copy[ch, k].start()
-        ref = held.at[x, c, :, held_cols(ch)]
-        a_copy[ch] = remote(ref, ref, ga_s.at[ch], ga_r.at[ch], c_peer)
-        a_copy[ch].start()
+        if ch not in CROSS_FIRST:
+            for s in range(2):
+                launch(functools.partial(stream, ch, 0, s), can_send(0, s))
+        launch(functools.partial(own_x, ch))
+
+    def gather_first(ch):
+        if ch in CROSS_FIRST:
+            own_x(ch).wait_recv()
+            for s in range(2):
+                launch(functools.partial(stream, ch, 0, s), can_send(0, s))
+
+    def gather_a(ch, h):
+        for s in range(2):
+            pl.when(can_recv(h, s))(lambda h=h, s=s: arrival(ch, h, s).wait_recv())
+            if h + 1 < end:
+                launch(functools.partial(stream, ch, h + 1, s), can_send(h + 1, s))
+            if ch not in CROSS_FIRST:
+                launch(functools.partial(forward_x, ch, h, s), can_recv(h, s))
+        if h + 1 == end:
+            launch(functools.partial(core_a, ch))
 
     def gather_b(ch):
-        for k in [0] + offsets:
-            x_copy[ch, k].wait_recv()
-        ref = held.at[1 - x, c, :, held_cols(ch)]
-        b_copy[ch] = remote(ref, ref, gb_s.at[ch], gb_r.at[ch], c_peer)
-        b_copy[ch].start()
+        if ch not in CROSS_FIRST:
+            own_x(ch).wait_recv()
+            for h, s in steps:
+                pl.when(can_recv(h, s))(lambda h=h, s=s: forward_x(ch, h, s).wait_recv())
+            launch(functools.partial(core_b, ch))
 
     def gather_c(ch):
-        a_copy[ch].wait_recv()
-        b_copy[ch].wait_recv()
+        core_a(ch).wait_recv()
+        if ch not in CROSS_FIRST:
+            core_b(ch).wait_recv()
         up_copies[ch].wait()
         cols = held[:, :, :, LANES + ch * size : LANES + (ch + 1) * size]
         term = jnp.dot(
@@ -214,13 +286,16 @@
         else:
             acc[...] += term
 
-    for i in range(NUM_CHUNKS + 2):
+    for i in range(NUM_CHUNKS + end + 1):
         if i < NUM_CHUNKS:
-            gather_a(i)
-        if 0 <= i - 1 < NUM_CHUNKS:
-            gather_b(i - 1)
-        if 0 <= i - 2:
-            gather_c(i - 2)
+            gather_first(i)
+        for h in range(end):
+            if 0 <= i - h < NUM_CHUNKS:
+                gather_a(i - h, h)
+        if 0 <= i - end < NUM_CHUNKS:
+            gather_b(i - end)
+        if 0 <= i - end - 1:
+            gather_c(i - end - 1)
 
     joined = acc[...]
     gate = joined[:, :width]
@@ -236,7 +311,15 @@
     other_weight = row_weights(1 - c)
     own_weight = row_weights(c)
     half = (2, wide_count * rows, size)
-    rc, rx, rz = {}, {}, {}
+
+    def rc(ch):
+        return remote(core_out.at[ch], core_in.at[ch], rc_s.at[ch], rc_r.at[ch], c_peer)
+
+    def rx(ch):
+        if ch in CROSS_FIRST:
+            at = CROSS_FIRST.index(ch)
+            return remote(last_out.at[at], last_in.at[at], rx_s.at[ch], rx_r.at[ch], x_peer)
+        return remote(x_out.at[ch], x_in.at[ch], rx_s.at[ch], rx_r.at[ch], x_peer)
 
     def scatter_a(ch):
         cols = slice(ch * size, (ch + 1) * size)
@@ -244,52 +327,100 @@
             hid[:, 1 - c].reshape(-1, width), down[:, cols], preferred_element_type=jnp.float32
         )
         core_out[ch] = (out * other_weight).astype(jnp.bfloat16).reshape(half)
-        rc[ch] = remote(core_out.at[ch], core_in.at[ch], rc_s.at[ch], rc_r.at[ch], c_peer)
-        rc[ch].start()
+        launch(functools.partial(rc, ch))
         out = jnp.dot(
             hid[:, c].reshape(-1, width), down[:, cols], preferred_element_type=jnp.float32
         )
         core_own[ch] = (out * own_weight).reshape(half)
 
     def scatter_b(ch):
-        rc[ch].wait_recv()
-        out = core_own[ch, 1 - x] + core_in[ch, 1 - x].astype(jnp.float32)
-        x_out[ch] = out.astype(jnp.bfloat16)
-        rx[ch] = remote(x_out.at[ch], x_in.at[ch], rx_s.at[ch], rx_r.at[ch], x_peer)
-        rx[ch].start()
-        x_own[ch] = core_own[ch, x] + core_in[ch, x].astype(jnp.float32)
-
-    def scatter_c(ch):
-        rx[ch].wait_recv()
-        out = x_own[ch] + x_in[ch].astype(jnp.float32)
-        x_own[ch] = out
-        z_out[ch] = out.astype(jnp.bfloat16)
-        for k in offsets:
-            rz[ch, k] = remote(
-                z_out.at[ch, block(z_peers[k])], z_in.at[ch, k - 1],
-                rz_s.at[ch, k], rz_r.at[ch, k], (part, z_peers[k], narrow),
-            )
-            rz[ch, k].start()
+        rc(ch).wait_recv()
+        if ch in CROSS_FIRST:
+            core_own[ch] += core_in[ch].astype(jnp.float32)
+        else:
+            out = core_own[ch, 1 - x] + core_in[ch, 1 - x].astype(jnp.float32)
+            x_out[ch] = out.astype(jnp.bfloat16)
+            launch(functools.partial(rx, ch))
+            x_own[ch] = core_own[ch, x] + core_in[ch, x].astype(jnp.float32)
+
+    def mine(ch, index):
+        if ch in CROSS_FIRST:
+            return core_own.at[ch, :, block(index)]
+        return x_own.at[ch, block(index)]
+
+    def slot(ref, ch, s, g):
+        return ref.at[ch, s, g] if ch in CROSS_FIRST else ref.at[ch, s, g, 0]
+
+    def rz(ch, s, g):
+        return remote(
+            slot(z_out, ch, s, g), slot(z_in, ch, s, g - 1),
+            rz_s.at[ch, s, g], rz_r.at[ch, s, g - 1], z_peer(s),
+        )
+
+    def rz_arrival(ch, s, g):
+        ref = slot(z_in, ch, s, g)
+        return remote(ref, ref, rz_s.at[ch, s, g], rz_r.at[ch, s, g], x_peer)
+
+    def scatter_c(ch, g):
+        if ch not in CROSS_FIRST and g == end:
+            rx(ch).wait_recv()
+            x_own[ch] += x_in[ch].astype(jnp.float32)
+        for s in range(2):
+            valid = z + g <= end if s == 0 else z >= g
+            before = has_low if s == 0 else has_high
+
+            def plain(g=g, s=s):
+                out = mine(ch, z + signs[s] * g)[...]
+                slot(z_out, ch, s, g)[...] = out.astype(jnp.bfloat16)
+
+            def added(g=g, s=s):
+                rz_arrival(ch, s, g).wait_recv()
+                out = mine(ch, z + signs[s] * g)[...]
+                out += slot(z_in, ch, s, g)[...].astype(jnp.float32)
+                slot(z_out, ch, s, g)[...] = out.astype(jnp.bfloat16)
+
+            pl.when(valid & jnp.logical_not(before))(plain)
+            if g < end:
+                pl.when(valid & before)(added)
+            launch(functools.partial(rz, ch, s, g), valid)
 
     def scatter_d(ch):
-        out = x_own[ch, block(z), :]
-        for k in offsets:
-            rz[ch, k].wait_recv()
-            out += z_in[ch, k - 1].astype(jnp.float32)
+        def add_in(s):
+            rz_arrival(ch, s, 0).wait_recv()
+            mine(ch, z)[...] += slot(z_in, ch, s, 0)[...].astype(jnp.float32)
+
+        pl.when(has_low)(lambda: add_in(0))
+        pl.when(has_high)(lambda: add_in(1))
+        cols = slice(ch * size, (ch + 1) * size)
+        if ch in CROSS_FIRST:
+            at = CROSS_FIRST.index(ch)
+            last_out[at] = core_own[ch, 1 - x, block(z), :].astype(jnp.bfloat16)
+            launch(functools.partial(rx, ch))
+        else:
+            out_ref[:, cols] = x_own[ch, block(z), :].astype(jnp.bfloat16)
+
+    def scatter_e(ch):
+        at = CROSS_FIRST.index(ch)
+        rx(ch).wait_recv()
+        out = core_own[ch, x, block(z), :] + last_in[at].astype(jnp.float32)
         out_ref[:, ch * size : (ch + 1) * size] = out.astype(jnp.bfloat16)
 
+    order = list(CROSS_FIRST) + [ch for ch in range(NUM_CHUNKS) if ch not in CROSS_FIRST]
     for i in range(NUM_CHUNKS + 1):
         if i < NUM_CHUNKS:
-            scatter_a(i)
+            scatter_a(order[i])
         if 0 <= i - 1:
-            scatter_b(i - 1)
-    for i in range(NUM_CHUNKS + 1):
-        if i < NUM_CHUNKS:
-            scatter_c(i)
-        if 0 <= i - 1:
-            scatter_d(i - 1)
-    for copy in sends:
-        copy.wait_send()
+            scatter_b(order[i - 1])
+    for i in range(NUM_CHUNKS + end):
+        for k in range(end):
+            if 0 <= i - k < NUM_CHUNKS:
+                scatter_c(order[i - k], end - k)
+        if 0 <= i - end:
+            scatter_d(order[i - end])
+    for ch in CROSS_FIRST:
+        scatter_e(ch)
+    for finish in sends:
+        finish()
 
 
 def dense_body(tokens, route_copy, gate_value, w_gate_up, w_down):
@@ -321,14 +452,16 @@
             pltpu.VMEM((n, col, size), bf16),
             pltpu.VMEM((n, col, size), bf16),
             pltpu.VMEM((n, col, size), f32),
-            pltpu.VMEM((n, col, size), bf16),
-            pltpu.VMEM((n, wide_count - 1, rows, size), bf16),
+            pltpu.VMEM((n, 2, wide_count, 2, rows, size), bf16),
+            pltpu.VMEM((n, 2, wide_count, 2, rows, size), bf16),
+            pltpu.VMEM((max(1, len(CROSS_FIRST)), rows, size), bf16),
+            pltpu.VMEM((max(1, len(CROSS_FIRST)), rows, size), bf16),
             dma((n,)), dma,
-            dma((n, wide_count)), dma((n, wide_count)),
-            dma((n, wide_count)), dma((n, wide_count)),
+            dma((n, 2, wide_count)), dma((n, 2, wide_count)),
+            dma((n, 3, wide_count)), dma((n, 3, wide_count)),
             dma((n,)), dma((n,)), dma((n,)), dma((n,)),
             dma((n,)), dma((n,)), dma((n,)), dma((n,)),
-            dma((n, wide_count)), dma((n, wide_count)),
+            dma((n, 2, wide_count)), dma((n, 2, wide_count)),
         ],
         compiler_params=pltpu.CompilerParams(
             collective_id=0, has_side_effects=True, vmem_limit_bytes=56 * 1024 * 1024
@@ -338,8 +471,8 @@
         ),
     )(
         tokens.reshape(rows, dim),
-        route_copy.reshape(rows, -1),
-        gate_value.reshape(rows, -1),
+        route_copy.transpose(0, 2, 1),
+        gate_value.transpose(0, 2, 1),
         w_gate_up[0],
         w_down[0],
     )

time: 70.4 us -> 65.3 us (0.928)
  local copies, waits for them, and re-layouts: 4.37 us -> 1.64 us
  Pallas kernels: 65.8 us -> 63.4 us
    reshape x2 -> x0, local copies, waits for them, and re-layouts: 2.73 us -> none  [the longest x1 1.36 us: dense_body(): route_copy.reshape(rows, -1)]
    pallas_call x1, Pallas kernels: 65.8 us -> 63.4 us  [dense_body(): pl.pallas_call(functools.partial(dense_kernel, wide_count), out_shape=jax...]
where the time goes in v2:
time: 65.3 us; the launch traced here: 65.1 us
  Pallas kernels  63.4 us (97%)
  local copies, waits for them, and re-layouts  1.64 us (3%)
    pallas_call x1, Pallas kernels, dense_body(): pl.pallas_call(functools.partial(dense_kernel, wide_count), out_shape=jax...  63.4 us
    unnamed x1, local copies, waits for them, and re-layouts  1.64 us

profile of v2, /device:TPU:0, one launch (start us, length us, event | category | flops | bytes accessed | tf_op | source)
XLA Modules:
  0.0 65.1 jit_solution(69411889929253037)
XLA Ops:
  0.0 63.4 %shard_map.55 = bf16[16,7168]{1,0:T(8,128)(2,1)} custom-call(bf16[16,7168]{1,0:T(8,128)(2,1)} %bitcast.9, s32[2,4,8]{2,1,0:T(4,128)} %bitcast.10, f32[2,4,8]{2,1,0:T(4,128)} %bitcast.11, bf16[7168,512]{1,0:T(8,128)(2,1)} %bitcast.6, bf16[256,7168]{1,0:T(8,128)(2,1)} %bitcast.7), custom_call_target="tpu_custom_call" | custom-call | flops 2818572288 | bytes 11010048 | tf_op jit(solution)/shard_map/pallas_call | solution.py:438
  63.5 1.6 %copy.7 = bf16[2,8,7168]{2,1,0:T(8,128)(2,1)} copy(bf16[2,8,7168]{2,1,0:T(8,128)(2,1)} %bitcast.8) | data formatting | bytes 458752

commit v3 on v2

--- a/solution.py
+++ b/solution.py
@@ -98,8 +98,12 @@
     return jnp.stack(results)
 
 
-NUM_CHUNKS = 4
+UNITS = (6, 9, 6, 7)
 CROSS_FIRST = (3,)
+DIRECT = (0, 1, 2)
+GATHER_ORDER = (0, 1, 2, 3)
+SCATTER_ORDER = (3, 0, 1, 2)
+NUM_CHUNKS = len(UNITS)
 LANES = 128
 THIRD = 32
 MESH = pl.DeviceIdType.MESH
@@ -115,7 +119,9 @@
     rows, dim = tok_ref.shape
     num_steps, top_count, tok_rows = route_ref.shape
     width = down.shape[0]
-    size = dim // NUM_CHUNKS
+    unit = dim // sum(UNITS)
+    sizes = [count * unit for count in UNITS]
+    starts = [sum(sizes[:ch]) for ch in range(NUM_CHUNKS)]
     part = lax.axis_index("parts")
     z = lax.axis_index("wide")
     narrow = lax.axis_index("narrow")
@@ -133,18 +139,21 @@
 
     def cols_of(ch):
         if ch == 0:
-            return pl.ds(0, LANES + size)
-        return pl.ds(LANES + ch * size, size)
+            return pl.ds(0, LANES + sizes[0])
+        return pl.ds(LANES + starts[ch], sizes[ch])
+
+    def span_of(ch):
+        return pl.ds(starts[ch], sizes[ch])
 
     def z_peer(s):
         return (part, z + signs[s], narrow)
 
-    up_copies = []
-    for ch in range(NUM_CHUNKS):
-        span = pl.ds(ch * size, size)
+    up_copies = {}
+    for ch in GATHER_ORDER:
+        span = span_of(ch)
         copy = pltpu.make_async_copy(up_hbm.at[span], up.at[span], up_sem.at[ch])
         copy.start()
-        up_copies.append(copy)
+        up_copies[ch] = copy
     down_copy = pltpu.make_async_copy(down_hbm, down, down_sem)
     down_copy.start()
 
@@ -153,8 +162,8 @@
     def greet(peer):
         pl.semaphore_signal(barrier, inc=1, device_id=peer, device_id_type=MESH)
 
-    pl.when(has_high)(lambda: greet(z_peer(0)))
-    pl.when(has_low)(lambda: greet(z_peer(1)))
+    for k in range(1, wide_count):
+        greet((part, lax.rem(z + k, wide_count), narrow))
     greet(x_peer)
     greet(c_peer)
 
@@ -180,7 +189,7 @@
     held[x, c, block(z), 0:LANES] = coded
     held[x, c, block(z), LANES:] = tok_ref[...]
 
-    pl.semaphore_wait(barrier, 2 + has_low.astype(jnp.int32) + has_high.astype(jnp.int32))
+    pl.semaphore_wait(barrier, wide_count + 1)
 
     sends = []
 
@@ -204,6 +213,11 @@
             go()
             sends.append(finish)
 
+    def flush(count):
+        for finish in sends[:count]:
+            finish()
+        del sends[:count]
+
     def can_recv(h, s):
         return z >= h + 1 if s == 0 else z + h + 1 <= end
 
@@ -242,7 +256,7 @@
         ref = held.at[1 - x, c, :, cols_of(ch)]
         return remote(ref, ref, gb_s.at[ch], gb_r.at[ch], c_peer)
 
-    for ch in range(NUM_CHUNKS):
+    for ch in GATHER_ORDER:
         if ch not in CROSS_FIRST:
             for s in range(2):
                 launch(functools.partial(stream, ch, 0, s), can_send(0, s))
@@ -276,27 +290,28 @@
         if ch not in CROSS_FIRST:
             core_b(ch).wait_recv()
         up_copies[ch].wait()
-        cols = held[:, :, :, LANES + ch * size : LANES + (ch + 1) * size]
+        cols = held[:, :, :, pl.ds(LANES + starts[ch], sizes[ch])]
         term = jnp.dot(
-            cols.reshape(-1, size), up[ch * size : (ch + 1) * size, :],
+            cols.reshape(-1, sizes[ch]), up[span_of(ch), :],
             preferred_element_type=jnp.float32,
         )
-        if ch == 0:
+        if ch == GATHER_ORDER[0]:
             acc[...] = term
         else:
             acc[...] += term
 
     for i in range(NUM_CHUNKS + end + 1):
         if i < NUM_CHUNKS:
-            gather_first(i)
+            gather_first(GATHER_ORDER[i])
         for h in range(end):
             if 0 <= i - h < NUM_CHUNKS:
-                gather_a(i - h, h)
+                gather_a(GATHER_ORDER[i - h], h)
         if 0 <= i - end < NUM_CHUNKS:
-            gather_b(i - end)
+            gather_b(GATHER_ORDER[i - end])
         if 0 <= i - end - 1:
-            gather_c(i - end - 1)
-
+            gather_c(GATHER_ORDER[i - end - 1])
+
+    gathered = len(sends)
     joined = acc[...]
     gate = joined[:, :width]
     value = gate / (1.0 + jnp.exp(-gate)) * joined[:, width:]
@@ -310,46 +325,49 @@
 
     other_weight = row_weights(1 - c)
     own_weight = row_weights(c)
-    half = (2, wide_count * rows, size)
+    col = wide_count * rows
 
     def rc(ch):
-        return remote(core_out.at[ch], core_in.at[ch], rc_s.at[ch], rc_r.at[ch], c_peer)
+        return remote(core_out.at[:, :, span_of(ch)], core_in.at[:, :, span_of(ch)], rc_s.at[ch], rc_r.at[ch], c_peer)
 
     def rx(ch):
         if ch in CROSS_FIRST:
-            at = CROSS_FIRST.index(ch)
-            return remote(last_out.at[at], last_in.at[at], rx_s.at[ch], rx_r.at[ch], x_peer)
-        return remote(x_out.at[ch], x_in.at[ch], rx_s.at[ch], rx_r.at[ch], x_peer)
+            return remote(last_out.at[:, span_of(ch)], last_in.at[:, span_of(ch)], rx_s.at[ch], rx_r.at[ch], x_peer)
+        return remote(x_out.at[:, span_of(ch)], x_in.at[:, span_of(ch)], rx_s.at[ch], rx_r.at[ch], x_peer)
 
     def scatter_a(ch):
-        cols = slice(ch * size, (ch + 1) * size)
+        cols = span_of(ch)
+        half = (2, col, sizes[ch])
         out = jnp.dot(
             hid[:, 1 - c].reshape(-1, width), down[:, cols], preferred_element_type=jnp.float32
         )
-        core_out[ch] = (out * other_weight).astype(jnp.bfloat16).reshape(half)
+        core_out[:, :, cols] = (out * other_weight).astype(jnp.bfloat16).reshape(half)
         launch(functools.partial(rc, ch))
         out = jnp.dot(
             hid[:, c].reshape(-1, width), down[:, cols], preferred_element_type=jnp.float32
         )
-        core_own[ch] = (out * own_weight).reshape(half)
+        core_own[:, :, cols] = (out * own_weight).reshape(half)
 
     def scatter_b(ch):
         rc(ch).wait_recv()
-        if ch in CROSS_FIRST:
-            core_own[ch] += core_in[ch].astype(jnp.float32)
+        cols = span_of(ch)
+        if ch in CROSS_FIRST:
+            core_own[:, :, cols] += core_in[:, :, cols].astype(jnp.float32)
         else:
-            out = core_own[ch, 1 - x] + core_in[ch, 1 - x].astype(jnp.float32)
-            x_out[ch] = out.astype(jnp.bfloat16)
+            out = core_own[1 - x, :, cols] + core_in[1 - x, :, cols].astype(jnp.float32)
+            x_out[:, cols] = out.astype(jnp.bfloat16)
             launch(functools.partial(rx, ch))
-            x_own[ch] = core_own[ch, x] + core_in[ch, x].astype(jnp.float32)
+            x_own[:, cols] = core_own[x, :, cols] + core_in[x, :, cols].astype(jnp.float32)
 
     def mine(ch, index):
         if ch in CROSS_FIRST:
-            return core_own.at[ch, :, block(index)]
-        return x_own.at[ch, block(index)]
+            return core_own.at[:, block(index), span_of(ch)]
+        return x_own.at[block(index), span_of(ch)]
 
     def slot(ref, ch, s, g):
-        return ref.at[ch, s, g] if ch in CROSS_FIRST else ref.at[ch, s, g, 0]
+        if ch in CROSS_FIRST:
+            return ref.at[s, g, :, :, span_of(ch)]
+        return ref.at[s, g, 0, :, span_of(ch)]
 
     def rz(ch, s, g):
         return remote(
@@ -357,6 +375,24 @@
             rz_s.at[ch, s, g], rz_r.at[ch, s, g - 1], z_peer(s),
         )
 
+    def rz_direct(ch, s, g):
+        return remote(
+            slot(z_out, ch, s, g), slot(z_in, ch, s, g - 1),
+            rz_s.at[ch, s, g], rz_r.at[ch, s, g - 1], (part, z + signs[s] * g, narrow),
+        )
+
+    def send_direct(ch):
+        for g in range(1, wide_count):
+            for s in range(2):
+                valid = z + g <= end if s == 0 else z >= g
+
+                def fill(g=g, s=s):
+                    out = mine(ch, z + signs[s] * g)[...]
+                    slot(z_out, ch, s, g)[...] = out.astype(jnp.bfloat16)
+
+                pl.when(valid)(fill)
+                launch(functools.partial(rz_direct, ch, s, g), valid)
+
     def rz_arrival(ch, s, g):
         ref = slot(z_in, ch, s, g)
         return remote(ref, ref, rz_s.at[ch, s, g], rz_r.at[ch, s, g], x_peer)
@@ -364,7 +400,11 @@
     def scatter_c(ch, g):
         if ch not in CROSS_FIRST and g == end:
             rx(ch).wait_recv()
-            x_own[ch] += x_in[ch].astype(jnp.float32)
+            x_own[:, span_of(ch)] += x_in[:, span_of(ch)].astype(jnp.float32)
+        if ch in DIRECT:
+            if g == end:
+                send_direct(ch)
+            return
         for s in range(2):
             valid = z + g <= end if s == 0 else z >= g
             before = has_low if s == 0 else has_high
@@ -385,33 +425,36 @@
             launch(functools.partial(rz, ch, s, g), valid)
 
     def scatter_d(ch):
-        def add_in(s):
-            rz_arrival(ch, s, 0).wait_recv()
-            mine(ch, z)[...] += slot(z_in, ch, s, 0)[...].astype(jnp.float32)
-
-        pl.when(has_low)(lambda: add_in(0))
-        pl.when(has_high)(lambda: add_in(1))
-        cols = slice(ch * size, (ch + 1) * size)
-        if ch in CROSS_FIRST:
-            at = CROSS_FIRST.index(ch)
-            last_out[at] = core_own[ch, 1 - x, block(z), :].astype(jnp.bfloat16)
+        def add_in(s, g):
+            rz_arrival(ch, s, g).wait_recv()
+            mine(ch, z)[...] += slot(z_in, ch, s, g)[...].astype(jnp.float32)
+
+        for g in range(end if ch in DIRECT else 1):
+            pl.when(z > g)(lambda g=g: add_in(0, g))
+            pl.when(z + g < end)(lambda g=g: add_in(1, g))
+        cols = span_of(ch)
+        if ch in CROSS_FIRST:
+            last_out[:, cols] = core_own[1 - x, block(z), cols].astype(jnp.bfloat16)
             launch(functools.partial(rx, ch))
         else:
-            out_ref[:, cols] = x_own[ch, block(z), :].astype(jnp.bfloat16)
+            out_ref[:, cols] = x_own[block(z), cols].astype(jnp.bfloat16)
 
     def scatter_e(ch):
-        at = CROSS_FIRST.index(ch)
         rx(ch).wait_recv()
-        out = core_own[ch, x, block(z), :] + last_in[at].astype(jnp.float32)
-        out_ref[:, ch * size : (ch + 1) * size] = out.astype(jnp.bfloat16)
-
-    order = list(CROSS_FIRST) + [ch for ch in range(NUM_CHUNKS) if ch not in CROSS_FIRST]
+        cols = span_of(ch)
+        out = core_own[x, block(z), cols] + last_in[:, cols].astype(jnp.float32)
+        out_ref[:, cols] = out.astype(jnp.bfloat16)
+
+    order = SCATTER_ORDER
     for i in range(NUM_CHUNKS + 1):
         if i < NUM_CHUNKS:
             scatter_a(order[i])
         if 0 <= i - 1:
             scatter_b(order[i - 1])
+    flush(gathered)
     for i in range(NUM_CHUNKS + end):
+        if i + 1 == NUM_CHUNKS + end:
+            flush(len(sends) - 2 * end)
         for k in range(end):
             if 0 <= i - k < NUM_CHUNKS:
                 scatter_c(order[i - k], end - k)
@@ -419,8 +462,7 @@
             scatter_d(order[i - end])
     for ch in CROSS_FIRST:
         scatter_e(ch)
-    for finish in sends:
-        finish()
+    flush(len(sends))
 
 
 def dense_body(tokens, route_copy, gate_value, w_gate_up, w_down):
@@ -428,7 +470,6 @@
     rows = num_steps * tok_rows
     wide_count = lax.axis_size("wide")
     width = w_down.shape[1]
-    size = dim // NUM_CHUNKS
     col = wide_count * rows
     bf16, f32 = jnp.bfloat16, jnp.float32
     vmem = pl.BlockSpec(memory_space=pltpu.VMEM)
@@ -446,16 +487,16 @@
             pltpu.VMEM((width, dim), bf16),
             pltpu.VMEM((4 * col, 2 * width), f32),
             pltpu.VMEM((2, 2, col, width), bf16),
-            pltpu.VMEM((n, 2, col, size), bf16),
-            pltpu.VMEM((n, 2, col, size), bf16),
-            pltpu.VMEM((n, 2, col, size), f32),
-            pltpu.VMEM((n, col, size), bf16),
-            pltpu.VMEM((n, col, size), bf16),
-            pltpu.VMEM((n, col, size), f32),
-            pltpu.VMEM((n, 2, wide_count, 2, rows, size), bf16),
-            pltpu.VMEM((n, 2, wide_count, 2, rows, size), bf16),
-            pltpu.VMEM((max(1, len(CROSS_FIRST)), rows, size), bf16),
-            pltpu.VMEM((max(1, len(CROSS_FIRST)), rows, size), bf16),
+            pltpu.VMEM((2, col, dim), bf16),
+            pltpu.VMEM((2, col, dim), bf16),
+            pltpu.VMEM((2, col, dim), f32),
+            pltpu.VMEM((col, dim), bf16),
+            pltpu.VMEM((col, dim), bf16),
+            pltpu.VMEM((col, dim), f32),
+            pltpu.VMEM((2, wide_count, 2, rows, dim), bf16),
+            pltpu.VMEM((2, wide_count, 2, rows, dim), bf16),
+            pltpu.VMEM((rows, dim), bf16),
+            pltpu.VMEM((rows, dim), bf16),
             dma((n,)), dma,
             dma((n, 2, wide_count)), dma((n, 2, wide_count)),
             dma((n, 3, wide_count)), dma((n, 3, wide_count)),
@@ -485,7 +526,8 @@
     copy_count = wide_count * narrow_count // SPLIT
     every_copy = route_copy.shape[2] == copy_count and copy_count <= THIRD
     whole_rows = tokens.shape[0] * tokens.shape[1] % 16 == 0
-    if every_copy and whole_rows and narrow_count == SPLIT:
+    whole_units = tokens.shape[2] % (sum(UNITS) * 128) == 0
+    if every_copy and whole_rows and whole_units and narrow_count == SPLIT:
         return dense_body(tokens, route_copy, gate_value, w_gate_up, w_down)
     return body(tokens, route_copy, gate_value, w_gate_up, w_down)
 

time: 65.3 us -> 63.9 us (0.979)
  Pallas kernels: 63.4 us -> 62.1 us
    pallas_call x1, Pallas kernels: 63.4 us -> 62.1 us  [dense_body(): pl.pallas_call(functools.partial(dense_kernel, wide_count), out_shape=jax...]
where the time goes in v3:
time: 63.9 us; the launch traced here: 63.7 us
  Pallas kernels  62.1 us (97%)
  local copies, waits for them, and re-layouts  1.64 us (3%)
    pallas_call x1, Pallas kernels, dense_body(): pl.pallas_call(functools.partial(dense_kernel, wide_count), out_shape=jax...  62.1 us
    unnamed x1, local copies, waits for them, and re-layouts  1.64 us

profile of v3, /device:TPU:0, one launch (start us, length us, event | category | flops | bytes accessed | tf_op | source)
XLA Modules:
  0.0 63.7 jit_solution(8788938880083682374)
XLA Ops:
  0.0 62.1 %shard_map.55 = bf16[16,7168]{1,0:T(8,128)(2,1)} custom-call(bf16[16,7168]{1,0:T(8,128)(2,1)} %bitcast.9, s32[2,4,8]{2,1,0:T(4,128)} %bitcast.10, f32[2,4,8]{2,1,0:T(4,128)} %bitcast.11, bf16[7168,512]{1,0:T(8,128)(2,1)} %bitcast.6, bf16[256,7168]{1,0:T(8,128)(2,1)} %bitcast.7), custom_call_target="tpu_custom_call" | custom-call | flops 2818572288 | bytes 11010048 | tf_op jit(solution)/shard_map/pallas_call | solution.py:479
  62.1 1.6 %copy.7 = bf16[2,8,7168]{2,1,0:T(8,128)(2,1)} copy(bf16[2,8,7168]{2,1,0:T(8,128)(2,1)} %bitcast.8) | data formatting | bytes 458752
